TPU v7x, 1024 devices: a whole 4x4x32 slice. The times are simulated.
1024 devices in a mesh: expert: 16 (over y, x), dp: 64 (over z, core).
Axes of the slice: x: 4, y: 4, z: 32, core: 2. Of those that a mesh axis runs over, the one named last changes fastest.
Arguments:
- tokens: bfloat16 [131072, 2048], P(('expert', 'dp')), may hold values from -6 to 6
- out_grad: bfloat16 [131072, 2048], P(('expert', 'dp')), may hold values from -6 to 6
- proj_in: bfloat16 [16, 2048, 512], P('expert'), may hold values from -0.125 to 0.125
- proj_out: bfloat16 [16, 512, 2048], P('expert'), may hold values from -0.25 to 0.25
- picked: int32 [1024, 16, 4], P(('expert', 'dp')), may hold values from 0 to 127, as said below
- gate_values: float32 [1024, 16, 4], P(('expert', 'dp')), may hold values from 0.1 to 1
Outputs:
- layer_out: bfloat16 [131072, 2048], P(('expert', 'dp'))
- token_grads: bfloat16 [131072, 2048], P(('expert', 'dp'))
- gate_grads: float32 [1024, 16, 4], P(('expert', 'dp'))
- grad_proj_in: float32 [16, 2048, 512], P('expert', 'dp')
Inputs may be any that keep to these rules, and one draw needn't show every extreme that they name: `picked`: for each group and expert the 4 entries are distinct positions among the group's 128 tokens.
All inputs are finite; a program needn't handle non-finite values.
Results may differ from a plain program's by a relative error of at most 0.0085.
Values may be sent and summed in bfloat16 or wider, within the bound.
A program may use at most 32 MiB of HBM per device.

v0:
```python
import math

import jax
import jax.numpy as jnp
from jax import lax
from jax.sharding import PartitionSpec as P


def gelu_parts(hidden_pre):
    normal_cdf = 0.5 * (1.0 + lax.erf(hidden_pre * (1.0 / math.sqrt(2.0))))
    density = jnp.exp(-0.5 * hidden_pre * hidden_pre) * (1.0 / math.sqrt(2.0 * math.pi))
    return (hidden_pre * normal_cdf, normal_cdf + hidden_pre * density)


def body(tokens, out_grad, proj_in, proj_out, picked, gate_values):
    group_count, expert_count, slot_count = picked.shape
    group_size = tokens.shape[0] // group_count
    width = tokens.shape[1]
    starts = (jnp.arange(group_count, dtype=jnp.int32) * group_size)[:, None, None]
    token_index = jnp.transpose(picked + starts, (1, 0, 2)).reshape(
        expert_count, group_count * slot_count
    )
    gate_rows = jnp.transpose(gate_values, (1, 0, 2)).reshape(
        expert_count, group_count * slot_count
    )
    rows_in = tokens[token_index]
    grad_rows = out_grad[token_index]
    scaled = (gate_rows[:, :, None] * grad_rows.astype(jnp.float32)).astype(jnp.bfloat16)
    received = lax.all_to_all(rows_in, "expert", split_axis=0, concat_axis=1, tiled=True)[0]
    weight_a = proj_in[0]
    weight_b = proj_out[0]
    hidden_pre = jnp.dot(received, weight_a, preferred_element_type=jnp.float32)
    activation, gelu_slope = gelu_parts(hidden_pre)
    hidden = activation.astype(jnp.bfloat16)
    expert_out = jnp.dot(hidden, weight_b, preferred_element_type=jnp.float32).astype(jnp.bfloat16)
    returned = lax.all_to_all(expert_out[None], "expert", split_axis=1, concat_axis=0, tiled=True)
    grad_recv = lax.all_to_all(scaled, "expert", split_axis=0, concat_axis=1, tiled=True)[0]
    back_act = jnp.einsum("rd,fd->rf", grad_recv, weight_b, preferred_element_type=jnp.float32)
    back_pre = (back_act * gelu_slope).astype(jnp.bfloat16)
    input_rows = jnp.einsum(
        "rf,df->rd", back_pre, weight_a, preferred_element_type=jnp.float32
    ).astype(jnp.bfloat16)
    term_in = jnp.einsum("rd,rf->df", received, back_pre, preferred_element_type=jnp.float32)[None]
    grad_proj_in = lax.psum_scatter(term_in, "dp", scatter_dimension=1, tiled=True)
    back_rows = lax.all_to_all(input_rows[None], "expert", split_axis=1, concat_axis=0, tiled=True)
    picks_hot = (picked[:, :, :, None] == jnp.arange(group_size, dtype=jnp.int32)).astype(
        jnp.float32
    )
    out_blocks = returned.reshape(expert_count, group_count, slot_count, width).astype(jnp.float32)
    layer_out = (
        jnp.einsum(
            "gect,egcd->gtd",
            picks_hot * gate_values[:, :, :, None],
            out_blocks,
            precision=lax.Precision.HIGHEST,
        )
        .reshape(tokens.shape)
        .astype(jnp.bfloat16)
    )
    gate_flat = jnp.sum(grad_rows.astype(jnp.float32) * returned.astype(jnp.float32), axis=2)
    gate_grads = jnp.transpose(gate_flat.reshape(expert_count, group_count, slot_count), (1, 0, 2))
    grad_blocks = back_rows.reshape(expert_count, group_count, slot_count, width).astype(
        jnp.float32
    )
    token_grads = (
        jnp.einsum("gect,egcd->gtd", picks_hot, grad_blocks, precision=lax.Precision.HIGHEST)
        .reshape(tokens.shape)
        .astype(jnp.bfloat16)
    )
    return (layer_out, token_grads, gate_grads, grad_proj_in)


def solution(mesh):
    return jax.shard_map(
        body,
        mesh=mesh,
        in_specs=(
            P(("expert", "dp"), None),
            P(("expert", "dp"), None),
            P("expert", None, None),
            P("expert", None, None),
            P(("expert", "dp"), None, None),
            P(("expert", "dp"), None, None),
        ),
        out_specs=(
            P(("expert", "dp"), None),
            P(("expert", "dp"), None),
            P(("expert", "dp"), None, None),
            P("expert", "dp", None),
        ),
        check_vma=False,
    )
```

profile of v0, /device:TPU:1, one launch (start us, length us, event | category | flops | bytes accessed | tf_op | source)
XLA Modules:
  0.0 268.0 jit_solution(7691457743380029182)
XLA Ops:
  7.2 0.0 copy-start
  7.2 0.8 compare_select_fusion
  8.0 0.1 copy.26
  8.1 0.1 reshape.100
  8.2 2.1 gather_fusion
  10.3 0.0 copy-start.3
  10.3 0.8 reshape.99
  11.1 7.6 %all-to-all-start = ((bf16[16,4,2048]{2,1,0:T(4,128)(2,1)}), bf16[16,4,2048]{2,1,0:T(4,128)(2,1)S(1)}, u32[]{:S(2)}, u32[]{:S(2)}) async-start(bf16[16,4,2048]{2,1,0:T(4,128)(2,1)} %reshape.99), calls=%async_computation | async-start | bytes 524288 | tf_op jit(solution)/shard_map/all_to_all | solution.py:29
  18.7 0.7 gather_fusion.1
  19.5 0.2 reshape.116
  19.7 0.1 copy.29
  19.8 0.9 multiply_convert_fusion
  20.6 5.7 %all-to-all-done = bf16[16,4,2048]{2,1,0:T(4,128)(2,1)S(1)} async-done(((bf16[16,4,2048]{2,1,0:T(4,128)(2,1)}), bf16[16,4,2048]{2,1,0:T(4,128)(2,1)S(1)}, u32[]{:S(2)}, u32[]{:S(2)}) %all-to-all-start) | async-done | bytes 262176 | tf_op jit(solution)/shard_map/all_to_all | solution.py:29
  26.3 3.5 %all-to-all-start.2 = ((bf16[16,4,2048]{2,1,0:T(4,128)(2,1)}), bf16[16,4,2048]{2,1,0:T(4,128)(2,1)S(1)}, u32[]{:S(2)}, u32[]{:S(2)}) async-start(bf16[16,4,2048]{2,1,0:T(4,128)(2,1)} %multiply_convert_fusion), calls=%async_computation.2 | async-start | bytes 524288 | tf_op jit(solution)/shard_map/all_to_all | solution.py:37
  29.8 0.0 reduce-scatter.2.cloned.1.call-start
  29.9 0.1 squeeze.12
  29.9 0.5 fusion.8
  30.4 7.8 %all-to-all-done.2 = bf16[16,4,2048]{2,1,0:T(4,128)(2,1)S(1)} async-done(((bf16[16,4,2048]{2,1,0:T(4,128)(2,1)}), bf16[16,4,2048]{2,1,0:T(4,128)(2,1)S(1)}, u32[]{:S(2)}, u32[]{:S(2)}) %all-to-all-start.2) | async-done | bytes 262176 | tf_op jit(solution)/shard_map/all_to_all | solution.py:37
  38.2 0.1 squeeze.15
  38.3 2.4 fusion.13
  40.6 2.7 convolution_bitcast_fusion
  43.3 0.0 reduce-scatter.2.cloned.1.call-update
  43.3 0.7 fusion.3
  44.1 0.4 copy.43
  44.5 0.5 broadcast.59
  45.0 2.2 reduce.6
  47.2 0.9 reshape.124
  48.1 3.5 %all-to-all-start.3 = ((bf16[16,2,4096]{2,1,0:T(2,128)(2,1)}), bf16[16,2,4096]{2,1,0:T(2,128)(2,1)S(1)}, u32[]{:S(2)}, u32[]{:S(2)}) async-start(bf16[16,2,4096]{2,1,0:T(2,128)(2,1)} %reshape.124), calls=%async_computation.3 | async-start | bytes 524288 | tf_op jit(solution)/shard_map/all_to_all | solution.py:45
  51.6 2.1 fusion.2
  53.7 0.4 copy.44
  54.1 2.2 reduce.5
  56.3 0.9 reshape.122
  57.2 1.9 all-to-all-done.3
  59.1 4.7 %all-to-all-start.1 = ((bf16[16,2,4096]{2,1,0:T(2,128)(2,1)}), bf16[16,2,4096]{2,1,0:T(2,128)(2,1)S(1)}, u32[]{:S(2)}, u32[]{:S(2)}) async-start(bf16[16,2,4096]{2,1,0:T(2,128)(2,1)} %reshape.122), calls=%async_computation.1 | async-start | bytes 524288 | tf_op jit(solution)/shard_map/all_to_all | solution.py:36
  63.8 0.3 reshape.125
  64.1 0.0 copy-start.2
  64.1 2.1 bitcast_reduce_fusion
  66.3 1.1 reshape.96
  67.3 5.0 %all-to-all-done.1 = bf16[16,2,4096]{2,1,0:T(2,128)(2,1)S(1)} async-done(((bf16[16,2,4096]{2,1,0:T(2,128)(2,1)}), bf16[16,2,4096]{2,1,0:T(2,128)(2,1)S(1)}, u32[]{:S(2)}, u32[]{:S(2)}) %all-to-all-start.1) | async-done | bytes 262176 | tf_op jit(solution)/shard_map/all_to_all | solution.py:36
  72.3 0.3 reshape.123
  72.6 2.1 bitcast_reduce_fusion.1
  74.7 1.1 reshape.95
  75.8 0.3 fusion.16
  76.1 0.1 transpose_reshape.3
  76.2 0.7 copy.33
  76.9 1.2 fusion.1
  78.1 1.5 fusion
  79.5 181.6 %reduce-scatter.2.cloned.1.call-done = f32[1,32,512]{2,1,0:T(8,128)} async-done(((f32[1,2048,512]{2,1,0:T(8,128)}), f32[1,32,512]{2,1,0:T(8,128)}) %reduce-scatter.2.cloned.1.call-update) | async-done | bytes 65552 | tf_op jit(solution)/shard_map/reduce_scatter | solution.py:44
  (6 shorter events, 0.0 us)
Async XLA Ops:
  7.2 22.8 %copy-start = (bf16[1,2048,512]{2,1,0:T(8,128)(2,1)S(1)}, bf16[1,2048,512]{2,1,0:T(8,128)(2,1)}, u32[]{:S(2)}) copy-start(bf16[1,2048,512]{2,1,0:T(8,128)(2,1)} %param.8) | copy-start | bytes 6291460
  7.2 11.6 %copy-start.1 = (bf16[128,2048]{1,0:T(8,128)(2,1)S(1)}, bf16[128,2048]{1,0:T(8,128)(2,1)}, u32[]{:S(2)}) copy-start(bf16[128,2048]{1,0:T(8,128)(2,1)} %param.7) | copy-start | bytes 1572868
  10.3 9.3 %copy-start.3 = (f32[1,16,4]{1,2,0:T(4,128)S(1)}, f32[1,16,4]{1,2,0:T(4,128)}, u32[]{:S(2)}) copy-start(f32[1,16,4]{1,2,0:T(4,128)} %param.11) | copy-start | bytes 772
  11.1 15.1 %all-to-all-start = ((bf16[16,4,2048]{2,1,0:T(4,128)(2,1)}), bf16[16,4,2048]{2,1,0:T(4,128)(2,1)S(1)}, u32[]{:S(2)}, u32[]{:S(2)}) async-start(bf16[16,4,2048]{2,1,0:T(4,128)(2,1)} %reshape.99), calls=%async_computation | async-start | bytes 524288 | tf_op jit(solution)/shard_map/all_to_all | solution.py:29
  26.3 11.9 %all-to-all-start.2 = ((bf16[16,4,2048]{2,1,0:T(4,128)(2,1)}), bf16[16,4,2048]{2,1,0:T(4,128)(2,1)S(1)}, u32[]{:S(2)}, u32[]{:S(2)}) async-start(bf16[16,4,2048]{2,1,0:T(4,128)(2,1)} %multiply_convert_fusion), calls=%async_computation.2 | async-start | bytes 524288 | tf_op jit(solution)/shard_map/all_to_all | solution.py:37
  29.8 231.3 %reduce-scatter.2.cloned.1.call-start = ((), (), s32[]{:S(2)}) async-start(), calls=%async_computation.5 | async-start | bytes 4259840 | tf_op jit(solution)/shard_map/reduce_scatter | solution.py:44
  48.1 11.0 %all-to-all-start.3 = ((bf16[16,2,4096]{2,1,0:T(2,128)(2,1)}), bf16[16,2,4096]{2,1,0:T(2,128)(2,1)S(1)}, u32[]{:S(2)}, u32[]{:S(2)}) async-start(bf16[16,2,4096]{2,1,0:T(2,128)(2,1)} %reshape.124), calls=%async_computation.3 | async-start | bytes 524288 | tf_op jit(solution)/shard_map/all_to_all | solution.py:45
  59.1 13.2 %all-to-all-start.1 = ((bf16[16,2,4096]{2,1,0:T(2,128)(2,1)}), bf16[16,2,4096]{2,1,0:T(2,128)(2,1)S(1)}, u32[]{:S(2)}, u32[]{:S(2)}) async-start(bf16[16,2,4096]{2,1,0:T(2,128)(2,1)} %reshape.122), calls=%async_computation.1 | async-start | bytes 524288 | tf_op jit(solution)/shard_map/all_to_all | solution.py:36
  64.1 12.8 %copy-start.2 = (s32[1,16,4]{1,2,0:T(4,128)S(1)}, s32[1,16,4]{1,2,0:T(4,128)}, u32[]{:S(2)}) copy-start(s32[1,16,4]{1,2,0:T(4,128)} %param.10) | copy-start | bytes 772
Sparse Core Ops, SparseCore 0:
  43.4 217.6 reduce-scatter.1
where the time goes:
time: 271 us; the launch traced here: 268 us
  waiting for transfers between devices  202 us (75%)
  starting transfers between devices  19.4 us (7%)
  local copies, waits for them, and re-layouts  15.1 us (6%)
  between operations  14.2 us (5%)
  matrix products  11 us (4%)
  other arithmetic  6.29 us (2%)
    reduce_scatter x1, waiting for transfers between devices, body(): lax.psum_scatter(term_in, 'dp', scatter_dimension=1, tiled=True)  182 us
    all_to_all x1, waiting for transfers between devices, body(): lax.all_to_all(scaled, 'expert', split_axis=0, concat_axis=1, tiled=True)[0]  7.78 us
    all_to_all x1, starting transfers between devices, body(): lax.all_to_all(rows_in, 'expert', split_axis=0, concat_axis=1, tiled=True)  7.58 us
    all_to_all x1, waiting for transfers between devices, body(): lax.all_to_all(rows_in, 'expert', split_axis=0, concat_axis=1, tiled=True)  5.65 us
  transfers between devices with their start and end apart: 5, of which 5 were waited for; matrix products, arithmetic and copies ran while one was open for 9% of the time, Pallas kernels for 0%

commit v1 on v0

v1 whole, which is shorter than its diff:
```python
import functools
import math

import jax
import jax.numpy as jnp
from jax import lax
from jax.experimental import pallas as pl
from jax.experimental.pallas import tpu as pltpu
from jax.sharding import PartitionSpec as P

MESH = pl.DeviceIdType.MESH
BF = jnp.bfloat16
F32 = jnp.float32
E, C, T, D, F = 16, 4, 128, 2048, 512
Q = 4
W = D // Q
MR = Q * C
RR = E * MR
R = E * C
NS = 2
CH = 32


def dot(a, b, dims=((1,), (0,)), precision=None):
    return lax.dot_general(a, b, (dims, ((), ())), preferred_element_type=F32, precision=precision)


def kernel(nz, picked_ref, gate_ref, tok_h, og_h, win_h, wout_h,
           lo_h, tg_h, gg_ref, gpi_ref,
           tok, og, win, wout, lo, tg,
           rows_s, rows_r, sc_s, sc_r, eo_s, eo_r, ir_s, ir_r, g_v,
           x_v, x_sib, xt, bp, perm, perm_t, a_hi, a_lo, a_one,
           cs, cr, ls, lr,
           ld_sem, st_sem, a2a_ss, a2a_rs, sib_ss, sib_rs, c_ss, c_rs, l_ss, l_rs):
    ns = nz // 4
    me = lax.axis_index("expert")
    dp = lax.axis_index("dp")
    z, h = dp // 2, dp % 2
    sib = z * 2 + (1 - h)

    def zdev(offset):
        return (me, lax.rem(z + offset + nz, nz) * 2 + h)

    loads = [pltpu.make_async_copy(s, d, ld_sem.at[i])
             for i, (s, d) in enumerate([(tok_h, tok), (og_h, og), (win_h, win), (wout_h, wout)])]
    for c in loads:
        c.start()

    barrier = pltpu.get_barrier_semaphore()

    def greet(k, _):
        pl.semaphore_signal(barrier, inc=1, device_id=(lax.rem(me + k, E), dp), device_id_type=MESH)
        return 0

    lax.fori_loop(1, E, greet, 0)
    pl.semaphore_signal(barrier, inc=1, device_id=(me, sib), device_id_type=MESH)
    for off in (1, -1, 2, -2):
        pl.semaphore_signal(barrier, inc=1, device_id=zdev(off), device_id_type=MESH)

    def iota(shape, dim):
        return lax.broadcasted_iota(jnp.int32, shape, dim)

    pickf = picked_ref[...].astype(F32)
    gatef = gate_ref[...]
    sel_e = ((iota((RR, E), 0) >> 4) == iota((RR, E), 1)).astype(F32)
    pk4 = dot(sel_e, pickf, precision=lax.Precision.HIGHEST)
    w4 = dot(sel_e, gatef, precision=lax.Precision.HIGHEST)
    is_c = (iota((RR, C), 0) & 3) == iota((RR, C), 1)
    pk = jnp.sum(jnp.where(is_c, pk4, 0.0), axis=1, keepdims=True)
    w = jnp.sum(jnp.where(is_c, w4, 0.0), axis=1, keepdims=True)
    tgt = pk.astype(jnp.int32) + ((iota((RR, 1), 0) >> 2) & 3) * T
    gather = (iota((RR, Q * T), 1) == tgt).astype(F32).astype(BF)
    diag = iota((RR, RR), 0) == iota((RR, RR), 1)
    tgt_row = jnp.sum(jnp.where(diag, tgt.astype(F32), 0.0), axis=0, keepdims=True).astype(jnp.int32)
    w_row = jnp.sum(jnp.where(diag, w, 0.0), axis=0, keepdims=True)

    def quarters(ref):
        return jnp.concatenate([ref[:, q * W:(q + 1) * W] for q in range(Q)], axis=0)

    def exchange(k, src, dst):
        def send(i, _):
            e = lax.rem(me + i, E)
            pltpu.make_async_remote_copy(
                src_ref=src.at[pl.ds(pl.multiple_of(e * MR, MR), MR)],
                dst_ref=dst.at[pl.ds(pl.multiple_of(me * MR, MR), MR)],
                send_sem=a2a_ss.at[k], recv_sem=a2a_rs.at[k],
                device_id=(e, dp), device_id_type=MESH).start()
            return 0
        lax.fori_loop(1, E, send, 0)
        own = pl.ds(pl.multiple_of(me * MR, MR), MR)
        dst[own, :] = src[own, :]

    def landed(k, dst):
        part = dst.at[pl.ds(0, (E - 1) * MR)]
        pltpu.make_async_copy(part, part, a2a_rs.at[k]).wait()

    def left(k, src):
        part = src.at[pl.ds(0, (E - 1) * MR)]
        pltpu.make_async_copy(part, part, a2a_ss.at[k]).wait()

    loads[0].wait()
    rows_s[...] = dot(gather, quarters(tok)).astype(BF)
    pl.semaphore_wait(barrier, E - 1 + 1 + 4)
    exchange(0, rows_s, rows_r)
    loads[1].wait()
    grad_rows = dot(gather, quarters(og))
    g_v[...] = grad_rows.astype(BF)
    sc_s[...] = (w * grad_rows).astype(BF)
    exchange(1, sc_s, sc_r)

    i0, i1 = iota((RR, RR), 0), iota((RR, RR), 1)
    to_q = ((i0 >> 2) & 15) * MR + (i0 >> 6) * C + (i0 & 3)
    perm[...] = (i1 == to_q).astype(F32).astype(BF)
    to_q_t = ((i1 >> 2) & 15) * MR + (i1 >> 6) * C + (i1 & 3)
    perm_t[...] = (i0 == to_q_t).astype(F32).astype(BF)
    hit = iota((Q * T, RR), 0) == tgt_row
    a_one[...] = hit.astype(F32).astype(BF)
    w_hi = w_row.astype(BF).astype(F32)
    a_hi[...] = jnp.where(hit, w_hi, 0.0).astype(BF)
    a_lo[...] = jnp.where(hit, w_row - w_hi, 0.0).astype(BF)

    landed(0, rows_r)
    x_v[...] = dot(perm[...], rows_r[...]).astype(BF)
    to_sib = pltpu.make_async_remote_copy(
        src_ref=x_v, dst_ref=x_sib, send_sem=sib_ss.at[0], recv_sem=sib_rs.at[0],
        device_id=(me, sib), device_id_type=MESH)
    to_sib.start()
    loads[2].wait()
    pre = jnp.zeros((R, F), F32)
    for q in range(Q):
        pre += dot(x_v[q * R:(q + 1) * R, :], win[q * W:(q + 1) * W, :])
    cdf = 0.5 * (1.0 + lax.erf(pre * (1.0 / math.sqrt(2.0))))
    density = jnp.exp(-0.5 * pre * pre) * (1.0 / math.sqrt(2.0 * math.pi))
    hidden = (pre * cdf).astype(BF)
    slope = cdf + pre * density
    landed(1, sc_r)
    scq = dot(perm[...], sc_r[...]).astype(BF)
    loads[3].wait()
    back = jnp.zeros((R, F), F32)
    for q in range(Q):
        back += dot(scq[q * R:(q + 1) * R, :], wout[:, q * W:(q + 1) * W], ((1,), (1,)))
    bp[0:R, :] = (back * slope).astype(BF)
    bp_sib = pltpu.make_async_remote_copy(
        src_ref=bp.at[pl.ds(0, R)], dst_ref=bp.at[pl.ds(R, R)], send_sem=sib_ss.at[1], recv_sem=sib_rs.at[1],
        device_id=(me, sib), device_id_type=MESH)
    bp_sib.start()

    to_sib.wait_recv()
    for q in range(Q):
        both = jnp.concatenate([x_v[q * R:(q + 1) * R, :], x_sib[q * R:(q + 1) * R, :]], axis=0)
        xt[q * W:(q + 1) * W, :] = both.T
    bp_sib.wait_recv()

    sub = F // NS

    def chunk(offset):
        t = lax.rem(z + offset + 2 * nz, nz)
        return xt[pl.ds(pl.multiple_of(t * (2 * CH) + h * CH, CH), CH), :]

    def chain(s, d, u):
        return pltpu.make_async_remote_copy(
            src_ref=cs.at[d, s, u], dst_ref=cr.at[d, s, u], send_sem=c_ss.at[d, s, u], recv_sem=c_rs.at[d, s, u],
            device_id=zdev(-2 if d else 2), device_id_type=MESH)

    def leaf(s, d, u):
        return pltpu.make_async_remote_copy(
            src_ref=ls.at[d, s, u], dst_ref=lr.at[d, s, u], send_sem=l_ss.at[d, s, u], recv_sem=l_rs.at[d, s, u],
            device_id=zdev(-1 if d else 1), device_id_type=MESH)

    half = nz // 2

    def send_leaves(s, d, own):
        for u in range(NS):
            ls[d, s, u] = own[:, u * sub:(u + 1) * sub].astype(BF)
            leaf(s, d, u).start()

    def first():
        own = dot(jnp.concatenate([chunk(half - 1), chunk(1 - half), chunk(half)], axis=0), bp[...])
        send_leaves(1, 0, own[0:CH])
        send_leaves(1, 1, own[CH:2 * CH])
        for u in range(NS):
            cs[0, 0, u] = own[2 * CH:, u * sub:(u + 1) * sub].astype(BF)
            chain(0, 0, u).start()

    def step(s, with_left_chain=True):
        own = dot(jnp.concatenate([chunk(half + 1 - 2 * (s + 1)), chunk(2 * (s + 1) - half - 1),
                                   chunk(half - 2 * s), chunk(2 * s - half)], axis=0), bp[...])
        send_leaves(s + 1, 0, own[0:CH])
        send_leaves(s + 1, 1, own[CH:2 * CH])
        for u in range(NS):
            for d in range(2):
                mine = own[(2 + d) * CH:(3 + d) * CH, u * sub:(u + 1) * sub]
                leaf(s, d, u).wait_recv()
                mine = mine + lr[d, s, u].astype(F32)
                if d == 0 or with_left_chain:
                    chain(s - 1, d, u).wait_recv()
                    mine = mine + cr[d, s - 1, u].astype(F32)
                cs[d, s, u] = mine.astype(BF)
                chain(s, d, u).start()

    def last():
        own = dot(chunk(0), bp[...])
        for u in range(NS):
            mine = own[:, u * sub:(u + 1) * sub]
            for d in range(2):
                leaf(ns, d, u).wait_recv()
                mine = mine + lr[d, ns, u].astype(F32)
                chain(ns - 1, d, u).wait_recv()
                mine = mine + cr[d, ns - 1, u].astype(F32)
            gpi_ref[:, u * sub:(u + 1) * sub] = mine

    first()

    eo = jnp.concatenate([dot(hidden, wout[:, q * W:(q + 1) * W]).astype(BF) for q in range(Q)], axis=0)
    eo_s[...] = dot(perm_t[...], eo).astype(BF)
    exchange(2, eo_s, eo_r)
    step(1, False)
    back_pre = bp[0:R, :]
    ir = jnp.concatenate(
        [dot(back_pre, win[q * W:(q + 1) * W, :], ((1,), (1,))).astype(BF) for q in range(Q)], axis=0)
    ir_s[...] = dot(perm_t[...], ir).astype(BF)
    exchange(3, ir_s, ir_r)
    step(2)
    landed(2, eo_r)
    prod = jnp.sum(g_v[...].astype(F32) * eo_r[...].astype(F32), axis=1, keepdims=True)
    sel_t = ((iota((E, RR), 1) >> 4) == iota((E, RR), 0)).astype(F32)
    gg_ref[...] = dot(sel_t, jnp.where(is_c, prod, 0.0), precision=lax.Precision.HIGHEST)
    step(3)
    for q in range(Q):
        lo[:, q * W:(q + 1) * W] = (dot(a_hi[q * T:(q + 1) * T, :], eo_r[...])
                                    + dot(a_lo[q * T:(q + 1) * T, :], eo_r[...])).astype(BF)
    st0 = pltpu.make_async_copy(lo, lo_h, st_sem.at[0])
    st0.start()
    step(4)
    landed(3, ir_r)
    for q in range(Q):
        tg[:, q * W:(q + 1) * W] = dot(a_one[q * T:(q + 1) * T, :], ir_r[...]).astype(BF)
    st1 = pltpu.make_async_copy(tg, tg_h, st_sem.at[1])
    st1.start()

    def loop(s, _):
        step(s)
        return 0

    lax.fori_loop(5, ns, loop, 0)
    last()

    st0.wait()
    st1.wait()
    to_sib.wait_send()
    bp_sib.wait_send()
    for k, buf in enumerate((rows_s, sc_s, eo_s, ir_s)):
        left(k, buf)

    def drain(s, _):
        for u in range(NS):
            for d in range(2):
                leaf(s, d, u).wait_send()

        @pl.when(s < ns)
        def _():
            for u in range(NS):
                for d in range(2):
                    chain(s, d, u).wait_send()
        return 0

    for u in range(NS):
        chain(0, 0, u).wait_send()
    lax.fori_loop(1, ns + 1, drain, 0)


def body(nz, tokens, out_grad, proj_in, proj_out, picked, gate_values):
    ns = nz // 4
    hbm = pl.BlockSpec(memory_space=pl.ANY)
    vmem = pl.BlockSpec(memory_space=pltpu.VMEM)
    buf = pltpu.VMEM((RR, W), BF)
    sub = F // NS
    red = pltpu.VMEM((2, ns + 1, NS, CH, sub), BF)
    dma = pltpu.SemaphoreType.DMA
    lo, tg, gg, gpi = pl.pallas_call(
        functools.partial(kernel, nz),
        out_shape=(
            jax.ShapeDtypeStruct((T, D), BF),
            jax.ShapeDtypeStruct((T, D), BF),
            jax.ShapeDtypeStruct((E, C), F32),
            jax.ShapeDtypeStruct((CH, F), F32),
        ),
        in_specs=[vmem, vmem, hbm, hbm, hbm, hbm],
        out_specs=(hbm, hbm, vmem, vmem),
        scratch_shapes=[
            pltpu.VMEM((T, D), BF), pltpu.VMEM((T, D), BF), pltpu.VMEM((D, F), BF), pltpu.VMEM((F, D), BF),
            pltpu.VMEM((T, D), BF), pltpu.VMEM((T, D), BF),
            buf, buf, buf, buf, buf, buf, buf, buf, buf,
            buf, buf, pltpu.VMEM((D, 2 * R), BF), pltpu.VMEM((2 * R, F), BF),
            pltpu.VMEM((RR, RR), BF), pltpu.VMEM((RR, RR), BF),
            pltpu.VMEM((Q * T, RR), BF), pltpu.VMEM((Q * T, RR), BF), pltpu.VMEM((Q * T, RR), BF),
            red, red, red, red,
            dma((4,)), dma((2,)), dma((4,)), dma((4,)), dma((2,)), dma((2,)),
            dma((2, ns + 1, NS)), dma((2, ns + 1, NS)), dma((2, ns + 1, NS)), dma((2, ns + 1, NS)),
        ],
        compiler_params=pltpu.CompilerParams(
            collective_id=0, has_side_effects=True, vmem_limit_bytes=40 * 1024 * 1024),
        name="moe_layer",
    )(picked[0], gate_values[0], tokens, out_grad, proj_in[0], proj_out[0])
    return lo, tg, gg[None], gpi[None]


def solution(mesh):
    return jax.shard_map(
        functools.partial(body, mesh.shape["dp"] // 2),
        mesh=mesh,
        in_specs=(
            P(("expert", "dp"), None),
            P(("expert", "dp"), None),
            P("expert", None, None),
            P("expert", None, None),
            P(("expert", "dp"), None, None),
            P(("expert", "dp"), None, None),
        ),
        out_specs=(
            P(("expert", "dp"), None),
            P(("expert", "dp"), None),
            P(("expert", "dp"), None, None),
            P("expert", "dp", None),
        ),
        check_vma=False,
    )
```

time: 271 us -> 75.2 us (0.28)
  the two profiles are of different devices: /device:TPU:1 before, /device:TPU:64 now
where the time goes in v1:
time: 75.2 us; the launch traced here: 74.9 us
  Pallas kernels  64.6 us (86%)
  local copies, waits for them, and re-layouts  9.65 us (13%)
    pallas_call x1, Pallas kernels, body(): pl.pallas_call(functools.partial(kernel, nz), out_shape=(jax.ShapeDtypeSt...  64.6 us
    unnamed x11, local copies, waits for them, and re-layouts  7.48 us

profile of v1, /device:TPU:64, one launch (start us, length us, event | category | flops | bytes accessed | tf_op | source)
XLA Modules:
  0.0 74.9 jit_solution(5836838786876904582)
XLA Ops:
  0.6 0.8 %copy.10.picked_ref = s32[16,4]{1,0:T(8,128)S(1)} copy(s32[16,4]{0,1:T(4,128)} %bitcast.9) | data formatting | bytes 512 | tf_op jit(solution)/shard_map/squeeze | solution.py:304
  1.4 0.8 %copy.11.gate_ref = f32[16,4]{1,0:T(8,128)S(1)} copy(f32[16,4]{0,1:T(4,128)} %bitcast.10) | data formatting | bytes 512 | tf_op jit(solution)/shard_map/squeeze | solution.py:304
  2.1 0.0 copy-start
  2.1 1.6 %copy-done = bf16[1,2048,512]{2,1,0:T(8,128)(2,1)S(1)} copy-done((bf16[1,2048,512]{2,1,0:T(8,128)(2,1)S(1)}, bf16[1,2048,512]{2,1,0:T(8,128)(2,1)}, u32[]{:S(2)}) %copy-start) | copy-done | bytes 2097176
  3.7 0.0 copy-start.1
  3.7 1.6 %copy-done.1 = bf16[1,512,2048]{2,1,0:T(8,128)(2,1)S(1)} copy-done((bf16[1,512,2048]{2,1,0:T(8,128)(2,1)S(1)}, bf16[1,512,2048]{2,1,0:T(8,128)(2,1)}, u32[]{:S(2)}) %copy-start.1) | copy-done | bytes 2097176
  5.3 0.0 copy-start.2
  5.3 1.0 %copy-done.2 = bf16[128,2048]{1,0:T(8,128)(2,1)S(1)} copy-done((bf16[128,2048]{1,0:T(8,128)(2,1)S(1)}, bf16[128,2048]{1,0:T(8,128)(2,1)}, u32[]{:S(2)}) %copy-start.2) | copy-done | bytes 524312
  6.4 0.0 copy-start.3
  6.4 1.0 %copy-done.3 = bf16[128,2048]{1,0:T(8,128)(2,1)S(1)} copy-done((bf16[128,2048]{1,0:T(8,128)(2,1)S(1)}, bf16[128,2048]{1,0:T(8,128)(2,1)}, u32[]{:S(2)}) %copy-start.3) | copy-done | bytes 524312
  7.4 64.6 %moe_layer.1 = (bf16[128,2048]{1,0:T(8,128)(2,1)S(1)}, bf16[128,2048]{1,0:T(8,128)(2,1)S(1)}, f32[16,4]{1,0:T(8,128)S(1)}, f32[32,512]{1,0:T(8,128)S(1)}) custom-call(s32[16,4]{1,0:T(8,128)S(1)} %copy.10.picked_ref, f32[16,4]{1,0:T(8,128)S(1)} %copy.11.gate_ref, bf16[128,2048]{1,0:T(8,128)(2,1)S(1)} %copy-done.2, bf16[128,2048]{1,0:T(8,128)(2,1)S(1)} %copy-done.3, ...), custom_call_target="tpu_custom_call" | custom-call | tf_op jit(solution)/shard_map/moe_layer/pallas_call | solution.py:280
  72.0 0.7 copy.12
  72.7 0.8 %copy.16 = bf16[128,2048]{1,0:T(8,128)(2,1)} copy(bf16[128,2048]{1,0:T(8,128)(2,1)S(1)} %get-tuple-element.16) | data formatting | bytes 1048576
  73.5 0.8 %copy.17 = bf16[128,2048]{1,0:T(8,128)(2,1)} copy(bf16[128,2048]{1,0:T(8,128)(2,1)S(1)} %get-tuple-element.17) | data formatting | bytes 1048576
  74.3 0.6 copy.18
Async XLA Ops:
  2.1 1.6 %copy-start = (bf16[1,2048,512]{2,1,0:T(8,128)(2,1)S(1)}, bf16[1,2048,512]{2,1,0:T(8,128)(2,1)}, u32[]{:S(2)}) copy-start(bf16[1,2048,512]{2,1,0:T(8,128)(2,1)} %param.8) | copy-start | bytes 6291460
  3.7 1.6 %copy-start.1 = (bf16[1,512,2048]{2,1,0:T(8,128)(2,1)S(1)}, bf16[1,512,2048]{2,1,0:T(8,128)(2,1)}, u32[]{:S(2)}) copy-start(bf16[1,512,2048]{2,1,0:T(8,128)(2,1)} %param.9) | copy-start | bytes 6291460
  5.3 1.0 %copy-start.2 = (bf16[128,2048]{1,0:T(8,128)(2,1)S(1)}, bf16[128,2048]{1,0:T(8,128)(2,1)}, u32[]{:S(2)}) copy-start(bf16[128,2048]{1,0:T(8,128)(2,1)} %tok_h.1) | copy-start | bytes 1572868
  6.4 1.0 %copy-start.3 = (bf16[128,2048]{1,0:T(8,128)(2,1)S(1)}, bf16[128,2048]{1,0:T(8,128)(2,1)}, u32[]{:S(2)}) copy-start(bf16[128,2048]{1,0:T(8,128)(2,1)} %og_h.1) | copy-start | bytes 1572868

commit v2 on v0

v2 whole, which is shorter than its diff:
```python
import functools
import math

import jax
import jax.numpy as jnp
from jax import lax
from jax.experimental import pallas as pl
from jax.experimental.pallas import tpu as pltpu
from jax.sharding import PartitionSpec as P

MESH = pl.DeviceIdType.MESH
BF = jnp.bfloat16
NT = ((1,), (1,))
F32 = jnp.float32
HIGH = lax.Precision.HIGHEST
E, C, T, D, F = 16, 4, 128, 2048, 512
Q = 4
W = D // Q
MR = Q * C
RR = E * MR
R = E * C
K = 2 * R
CH = 64
NS = 2
SR = CH // NS
GAPS = ((2, 3, 4, 7), (2, 3, 4, 6))
LANE, EXPRESS, PER_CHIP = 2.3, 1.6, 0.64


def side_plan(gaps):
    stops = [sum(gaps)]
    for g in gaps:
        stops.append(stops[-1] - g)
    roles, ready = {}, {}
    for d in range(stops[0], -1, -1):
        lane = d + 1 <= stops[0] and d + 1 not in stops
        at = ready[d + 1] + LANE if lane else 0.0
        express = d in stops and d != stops[0]
        hop = 1
        if express:
            last = stops[stops.index(d) - 1]
            at = max(at, ready[last] + EXPRESS + PER_CHIP * (last - d))
        if d in stops and d > 0:
            hop = d - stops[stops.index(d) + 1]
        ready[d] = at
        roles[d] = (lane, last if express else None, hop, at)
    return roles


PLANS = tuple(side_plan(g) for g in GAPS)
ORDER = sorted(((PLANS[s][d][3], -d, s) for s in range(2) for d in PLANS[s] if d > 0))
OFFSETS = sorted({1} | set(GAPS[0]) | set(GAPS[1]))
SLOTS = max(sum(g) for g in GAPS) + 1


def dot(a, b, dims=((1,), (0,)), precision=None):
    return lax.dot_general(a, b, (dims, ((), ())), preferred_element_type=F32, precision=precision)


def iota(shape, dim):
    return lax.broadcasted_iota(jnp.int32, shape, dim)


def kernel(nz, picked_h, gate_h, tok_h, og_h, win_h, wout_h,
           lo, tg, gg, gpi_o,
           picked, gate, tok, og, win, wout, gpi,
           rows_s, sc_s, rows_r, sc_r, eo_s, ir_s, eo_r, ir_r, g_v,
           x_v, xt, hid, bp, perm, perm_t, a_hi, a_lo, a_one, ms, mr,
           ld_sem, in_ss, in_rs, out_ss, out_rs, sib_ss, sib_rs, m_ss, m_rs):
    me = lax.axis_index("expert")
    dp = lax.axis_index("dp")
    z, h = dp // 2, dp % 2
    even, odd = z * 2, z * 2 + 1

    def zdev(offset):
        return (me, lax.rem(z + offset + nz, nz) * 2 + h)

    barrier = pltpu.get_barrier_semaphore()

    def signal(dev):
        pl.semaphore_signal(barrier, inc=1, device_id=dev, device_id_type=MESH)

    def greet(k, _):
        e = lax.rem(me + k, E)
        signal((e, odd))
        signal((e, even))
        return 0

    lax.fori_loop(1, E, greet, 0)
    signal((me, z * 2 + (1 - h)))

    @pl.when(h == 1)
    def _():
        for off in OFFSETS:
            signal(zdev(off))
            signal(zdev(-off))

    pairs = [(picked_h, picked), (gate_h, gate), (tok_h, tok), (og_h, og), (win_h, win), (wout_h, wout)]
    loads = [pltpu.make_async_copy(s, d, ld_sem.at[i]) for i, (s, d) in enumerate(pairs)]
    for c in loads:
        c.start()

    sel_e = ((iota((RR, E), 0) >> 4) == iota((RR, E), 1)).astype(F32)
    is_c = (iota((RR, C), 0) & 3) == iota((RR, C), 1)
    diag = iota((RR, RR), 0) == iota((RR, RR), 1)
    loads[0].wait()
    loads[1].wait()
    pk4 = dot(sel_e, picked[...].astype(F32), NT, HIGH)
    w4 = dot(sel_e, gate[...], NT, HIGH)
    pk = jnp.sum(jnp.where(is_c, pk4, 0.0), axis=1, keepdims=True)
    w = jnp.sum(jnp.where(is_c, w4, 0.0), axis=1, keepdims=True)
    tgt = pk.astype(jnp.int32) + ((iota((RR, 1), 0) >> 2) & 3) * T
    gather = (iota((RR, Q * T), 1) == tgt).astype(F32).astype(BF)

    def quarters(ref):
        return jnp.concatenate([ref[:, q * W:(q + 1) * W] for q in range(Q)], axis=0)

    def block(i, base=0):
        return pl.ds(pl.multiple_of(base + i * MR, MR), MR)

    def send_in(k, src, dst):
        def copy(e):
            return pltpu.make_async_remote_copy(
                src_ref=src.at[block(e)], dst_ref=dst.at[block(me, h * RR)],
                send_sem=in_ss.at[k], recv_sem=in_rs.at[k, h],
                device_id=(e, odd), device_id_type=MESH)

        def send(i, _):
            copy(lax.rem(me + i, E)).start()
            return 0

        lax.fori_loop(1, E, send, 0)

        @pl.when(h == 0)
        def _():
            copy(me).start()

        @pl.when(h == 1)
        def _():
            dst[block(me, RR), :] = src[block(me), :]

    def wait_rows(ref, start, count, sem):
        part = ref.at[pl.ds(start, count)]
        pltpu.make_async_copy(part, part, sem).wait()

    loads[2].wait()
    rows_s[...] = dot(gather, quarters(tok)).astype(BF)

    @pl.when(h == 0)
    def _():
        pl.semaphore_wait(barrier, 2 * E - 1)

    @pl.when(h == 1)
    def _():
        pl.semaphore_wait(barrier, 2 * E - 1 + 2 * len(OFFSETS))

    send_in(0, rows_s, rows_r)
    loads[3].wait()
    grad_rows = dot(gather, quarters(og))
    sc_s[...] = (w * grad_rows).astype(BF)
    send_in(1, sc_s, sc_r)
    g_v[...] = grad_rows.astype(BF)

    i0, i1 = iota((RR, RR), 0), iota((RR, RR), 1)
    to_q = ((i0 >> 2) & 15) * MR + (i0 >> 6) * C + (i0 & 3)
    perm[...] = (i1 == to_q).astype(F32).astype(BF)
    to_q_t = ((i1 >> 2) & 15) * MR + (i1 >> 6) * C + (i1 & 3)
    perm_t[...] = (i0 == to_q_t).astype(F32).astype(BF)
    tgt_row = jnp.sum(jnp.where(diag, tgt.astype(F32), 0.0), axis=0, keepdims=True).astype(jnp.int32)
    w_row = jnp.sum(jnp.where(diag, w, 0.0), axis=0, keepdims=True)
    hit = iota((Q * T, RR), 0) == tgt_row
    a_one[...] = hit.astype(F32).astype(BF)
    w_hi = w_row.astype(BF).astype(F32)
    a_hi[...] = jnp.where(hit, w_hi, 0.0).astype(BF)
    a_lo[...] = jnp.where(hit, w_row - w_hi, 0.0).astype(BF)

    def combine_out():
        for q in range(Q):
            a = slice(q * T, (q + 1) * T)
            lo[:, q * W:(q + 1) * W] = (dot(a_hi[a, :], eo_r[...]) + dot(a_lo[a, :], eo_r[...])).astype(BF)
        prod = jnp.sum(g_v[...].astype(F32) * eo_r[...].astype(F32), axis=1, keepdims=True)
        sel_t = ((iota((E, RR), 1) >> 4) == iota((E, RR), 0)).astype(F32)
        prod_row = jnp.sum(jnp.where(diag, prod, 0.0), axis=0, keepdims=True)
        by_c = jnp.where((iota((C, RR), 1) & 3) == iota((C, RR), 0), prod_row, 0.0)
        gg[...] = dot(by_c, sel_t, NT, HIGH)

    def combine_grad():
        for q in range(Q):
            tg[:, q * W:(q + 1) * W] = dot(a_one[q * T:(q + 1) * T, :], ir_r[...]).astype(BF)

    def to_sib(i, src, dst):
        return pltpu.make_async_remote_copy(
            src_ref=src, dst_ref=dst, send_sem=sib_ss.at[i], recv_sem=sib_rs.at[i],
            device_id=(me, z * 2 + (1 - h)), device_id_type=MESH)

    hid_copy = to_sib(0, hid, hid)
    bp_copy = to_sib(1, bp, bp)
    gpi_copy = to_sib(2, gpi, gpi_o)

    def by_quarter(src, dst):
        for cs in range(2):
            xs = dot(perm[...], src[cs * RR:(cs + 1) * RR, :]).astype(BF)
            for q in range(Q):
                dst[q, cs * R:(cs + 1) * R, :] = xs[q * R:(q + 1) * R, :]

    @pl.when(h == 1)
    def _():
        wait_rows(rows_r, 0, RR, in_rs.at[0, 0])
        wait_rows(rows_r, RR, RR - MR, in_rs.at[0, 1])
        by_quarter(rows_r, x_v)
        loads[4].wait()
        pre = dot(x_v[0], win[0:W, :])
        for q in range(1, Q):
            pre += dot(x_v[q], win[q * W:(q + 1) * W, :])
        cdf = 0.5 * (1.0 + lax.erf(pre * (1.0 / math.sqrt(2.0))))
        hid[...] = (pre * cdf).astype(BF)
        hid_copy.start()
        slope = cdf + pre * (jnp.exp(-0.5 * pre * pre) * (1.0 / math.sqrt(2.0 * math.pi)))
        for q in range(Q):
            xt[q * W:(q + 1) * W, :] = x_v[q].T
        loads[5].wait()
        wait_rows(sc_r, 0, RR, in_rs.at[1, 0])
        wait_rows(sc_r, RR, RR - MR, in_rs.at[1, 1])
        by_quarter(sc_r, x_v)
        back = dot(x_v[0], wout[:, 0:W], NT)
        for q in range(1, Q):
            back += dot(x_v[q], wout[:, q * W:(q + 1) * W], NT)
        bp[...] = (back * slope).astype(BF)
        bp_copy.start()

        def own(s, d):
            t = lax.rem(z + (d if s == 0 else -d) + nz, nz)
            return dot(xt[pl.ds(pl.multiple_of(t * CH, CH), CH), :], bp[...])

        def message(s, d, u):
            hop = PLANS[s][d][2]
            part = pl.ds(u * SR, SR)
            return pltpu.make_async_remote_copy(
                src_ref=ms.at[s, d, part], dst_ref=mr.at[s, d, part],
                send_sem=m_ss.at[s, d, u], recv_sem=m_rs.at[s, d, u],
                device_id=zdev(hop if s == 0 else -hop), device_id_type=MESH)

        def add(total, s, d, u):
            message(s, d, u).wait_recv()
            return total + mr[s, d, u * SR:(u + 1) * SR, :].astype(F32)

        def gathered(total, s, d, u):
            lane, last, _, _ = PLANS[s][d]
            if lane:
                total = add(total, s, d + 1, u)
            if last is not None:
                total = add(total, s, last, u)
            return total

        def role(s, d):
            mine = own(s, d)
            for u in range(NS):
                total = gathered(mine[u * SR:(u + 1) * SR], s, d, u)
                ms[s, d, u * SR:(u + 1) * SR, :] = total.astype(BF)
                message(s, d, u).start()

        for _, nd, s in ORDER:
            role(s, -nd)

        wait_rows(eo_r, 0, RR, out_rs.at[0])
        combine_out()
        wait_rows(ir_r, 0, RR, out_rs.at[1])
        combine_grad()

        mine = own(0, 0)
        for u in range(NS):
            total = mine[u * SR:(u + 1) * SR]
            for s in range(2):
                total = gathered(total, s, 0, u)
            for i in range(u * SR, (u + 1) * SR, min(SR, CH // 2)):
                part = total[i - u * SR:i - u * SR + min(SR, CH // 2)]
                if i < CH // 2:
                    gpi[i:i + part.shape[0], :] = part
                else:
                    gpi_o[i - CH // 2:i - CH // 2 + part.shape[0], :] = part
            if (u + 1) * SR == max(SR, CH // 2):
                gpi_copy.start()
        wait_rows(rows_s, 0, RR - MR, in_ss.at[0])
        wait_rows(sc_s, 0, RR - MR, in_ss.at[1])
        hid_copy.wait_send()
        bp_copy.wait_send()
        for s in range(2):
            for d in PLANS[s]:
                if d > 0:
                    for u in range(NS):
                        message(s, d, u).wait_send()
        gpi_copy.wait_send()

    @pl.when(h == 0)
    def _():
        def send_out(k, src, dst):
            def copy(cs, e):
                return pltpu.make_async_remote_copy(
                    src_ref=src.at[block(e, cs * RR)], dst_ref=dst.at[block(me)],
                    send_sem=out_ss.at[k, cs], recv_sem=out_rs.at[k],
                    device_id=(e, z * 2 + cs), device_id_type=MESH)

            def send(i, _):
                e = lax.rem(me + i, E)
                copy(1, e).start()
                copy(0, e).start()
                return 0

            lax.fori_loop(1, E, send, 0)
            copy(1, me).start()
            dst[block(me), :] = src[block(me), :]

        def by_source(parts, dst):
            for cs in range(2):
                rows = jnp.concatenate([p[cs * R:(cs + 1) * R] for p in parts], axis=0)
                dst[cs * RR:(cs + 1) * RR, :] = dot(perm_t[...], rows).astype(BF)

        loads[4].wait()
        loads[5].wait()
        hid_copy.wait_recv()
        by_source([dot(hid[...], wout[:, q * W:(q + 1) * W]).astype(BF) for q in range(Q)], eo_s)
        send_out(0, eo_s, eo_r)
        bp_copy.wait_recv()
        by_source([dot(bp[...], win[q * W:(q + 1) * W, :], NT).astype(BF) for q in range(Q)], ir_s)
        send_out(1, ir_s, ir_r)
        wait_rows(eo_r, 0, RR - MR, out_rs.at[0])
        combine_out()
        wait_rows(ir_r, 0, RR - MR, out_rs.at[1])
        combine_grad()
        wait_rows(rows_s, 0, RR, in_ss.at[0])
        wait_rows(sc_s, 0, RR, in_ss.at[1])
        for k, src in enumerate((eo_s, ir_s)):
            wait_rows(src, 0, RR - MR, out_ss.at[k, 0])
            wait_rows(src, 0, RR, out_ss.at[k, 1])
        gpi_copy.wait_recv()


def copy_out(a, b, c, d, oa, ob, oc, od, sem):
    copies = [pltpu.make_async_copy(s, t, sem.at[i]) for i, (s, t) in enumerate(((a, oa), (b, ob), (c, oc), (d, od)))]
    for x in copies:
        x.start()
    for x in copies:
        x.wait()


def body(nz, tokens, out_grad, proj_in, proj_out, picked, gate_values):
    hbm = pl.BlockSpec(memory_space=pltpu.HBM)
    vmem = pl.BlockSpec(memory_space=pltpu.VMEM)
    dma = pltpu.SemaphoreType.DMA

    def buf(*shape, dtype=BF):
        return pltpu.VMEM(shape, dtype)

    shapes = (
        jax.ShapeDtypeStruct((T, D), BF),
        jax.ShapeDtypeStruct((T, D), BF),
        jax.ShapeDtypeStruct((C, E), F32),
        jax.ShapeDtypeStruct((CH // 2, F), F32),
    )
    outs = pl.pallas_call(
        functools.partial(kernel, nz),
        out_shape=shapes,
        in_specs=[hbm] * 6,
        out_specs=(vmem,) * 4,
        scratch_shapes=[
            buf(C, E, dtype=jnp.int32), buf(C, E, dtype=F32), buf(T, D), buf(T, D), buf(D, F), buf(F, D),
            buf(CH // 2, F, dtype=F32),
            buf(RR, W), buf(RR, W), buf(2 * RR, W), buf(2 * RR, W), buf(2 * RR, W), buf(2 * RR, W),
            buf(RR, W), buf(RR, W), buf(RR, W),
            buf(Q, K, W), buf(D, K), buf(K, F), buf(K, F), buf(RR, RR), buf(RR, RR),
            buf(Q * T, RR), buf(Q * T, RR), buf(Q * T, RR),
            buf(2, SLOTS, CH, F), buf(2, SLOTS, CH, F),
            dma((6,)), dma((2,)), dma((2, 2)), dma((2, 2)), dma((2,)), dma((3,)), dma((3,)),
            dma((2, SLOTS, NS)), dma((2, SLOTS, NS)),
        ],
        compiler_params=pltpu.CompilerParams(
            collective_id=0, has_side_effects=True, vmem_limit_bytes=60 * 1024 * 1024),
        name="moe_layer",
    )(picked[0].T, gate_values[0].T, tokens, out_grad, proj_in[0], proj_out[0])
    lo, tg, gg, gpi = pl.pallas_call(
        copy_out, out_shape=shapes, in_specs=[vmem] * 4, out_specs=(hbm,) * 4,
        scratch_shapes=[dma((4,))], name="copy_out",
    )(*outs)
    return lo, tg, gg.T[None], gpi[None]


def solution(mesh):
    return jax.shard_map(
        functools.partial(body, mesh.shape["dp"] // 2),
        mesh=mesh,
        in_specs=(
            P(("expert", "dp"), None),
            P(("expert", "dp"), None),
            P("expert", None, None),
            P("expert", None, None),
            P(("expert", "dp"), None, None),
            P(("expert", "dp"), None, None),
        ),
        out_specs=(
            P(("expert", "dp"), None),
            P(("expert", "dp"), None),
            P(("expert", "dp"), None, None),
            P("expert", "dp", None),
        ),
        check_vma=False,
    )
```

time: 271 us -> 63.7 us (0.24)
  waiting for transfers between devices: 202 us -> 0 us
  Pallas kernels: 0 us -> 61.9 us
  starting transfers between devices: 19.4 us -> 0 us
  local copies, waits for them, and re-layouts: 15.1 us -> 0 us
  between operations: 14.2 us -> 0.64 us
  matrix products: 11 us -> 0 us
  other arithmetic: 6.29 us -> 0 us
    reduce_scatter x1 -> x0, waiting for transfers between devices: 182 us -> none  [body(): lax.psum_scatter(term_in, 'dp', scatter_dimension=1, tiled=True)]
    pallas_call x0 -> x2, Pallas kernels: none -> 61.9 us  [the longest x1 59.7 us: body(): pl.pallas_call(functools.partial(kernel, nz), out_shape=shapes, in_specs=...]
    all_to_all x4 -> x0, waiting for transfers between devices: 20.4 us -> none  [the longest x1 7.78 us: body(): lax.all_to_all(scaled, 'expert', split_axis=0, concat_axis=1, tiled=True)[0]]
    all_to_all x4 -> x0, starting transfers between devices: 19.3 us -> none  [the longest x1 7.58 us: body(): lax.all_to_all(rows_in, 'expert', split_axis=0, concat_axis=1, tiled=True)]
    dot_general x7 -> x0, matrix products: 11 us -> none  [the longest x1 2.66 us: body(): jnp.einsum('rd,rf->df', received, back_pre, preferred_element_type=jnp.fl...]
    unnamed x2 -> x0, other arithmetic: 4.31 us -> none
    all_to_all x2 -> x0, local copies, waits for them, and re-layouts: 4.3 us -> none  [the longest x1 2.15 us: body(): lax.all_to_all(input_rows[None], 'expert', split_axis=1, concat_axis=0, t...]
    gather x3 -> x0, local copies, waits for them, and re-layouts: 3.65 us -> none  [the longest x2 2.9 us: body(): rows_in = tokens[token_index]]
  transfers between devices with their start and end apart: 5 -> 0, of which waited for: 5 -> 0; matrix products, arithmetic and copies ran while one was open for 9% -> 0% of each run, Pallas kernels for 0% -> 0%
where the time goes in v2:
time: 63.7 us; the launch traced here: 62.5 us
  Pallas kernels  61.9 us (97%)
  between operations  0.64 us (1%)
    pallas_call x1, Pallas kernels, body(): pl.pallas_call(functools.partial(kernel, nz), out_shape=shapes, in_specs=...  59.7 us
    pallas_call x1, Pallas kernels, body(): pl.pallas_call(copy_out, out_shape=shapes, in_specs=[vmem] * 4, out_specs...  2.22 us

profile of v2, /device:TPU:1, one launch (start us, length us, event | category | flops | bytes accessed | tf_op | source)
XLA Modules:
  0.0 62.5 jit_solution(14657580891288374295)
XLA Ops:
  0.6 59.7 %moe_layer.1 = (bf16[128,2048]{1,0:T(8,128)(2,1)}, bf16[128,2048]{1,0:T(8,128)(2,1)}, f32[4,16]{1,0:T(4,128)}, f32[32,512]{1,0:T(8,128)}) custom-call(s32[4,16]{1,0:T(4,128)} %bitcast.14, f32[4,16]{1,0:T(4,128)} %bitcast.15, bf16[128,2048]{1,0:T(8,128)(2,1)} %tok_h.1, bf16[128,2048]{1,0:T(8,128)(2,1)} %og_h.1, bf16[2048,512]{1,0:T(8,128)(2,1)} %bitcast.12, ...), custom_call_target="tpu_custom_call" | custom-call | tf_op jit(solution)/shard_map/moe_layer/pallas_call | solution.py:360
  60.3 2.2 %copy_out.1 = (bf16[128,2048]{1,0:T(8,128)(2,1)}, bf16[128,2048]{1,0:T(8,128)(2,1)}, f32[4,16]{1,0:T(4,128)}, f32[32,512]{1,0:T(8,128)}) custom-call(bf16[128,2048]{1,0:T(8,128)(2,1)} %get-tuple-element.12.a, bf16[128,2048]{1,0:T(8,128)(2,1)} %get-tuple-element.13.b, f32[4,16]{1,0:T(4,128)} %get-tuple-element.14.c, f32[32,512]{1,0:T(8,128)} %get-tuple-element.15.d), custom_call_target="tpu_custom_call" | custom-call | tf_op jit(solution)/shard_map/copy_out/pallas_call | solution.py:380

commit v3 on v2

--- a/solution.py
+++ b/solution.py
@@ -23,34 +23,13 @@
 CH = 64
 NS = 2
 SR = CH // NS
-GAPS = ((2, 3, 4, 7), (2, 3, 4, 6))
-LANE, EXPRESS, PER_CHIP = 2.3, 1.6, 0.64
-
-
-def side_plan(gaps):
-    stops = [sum(gaps)]
-    for g in gaps:
-        stops.append(stops[-1] - g)
-    roles, ready = {}, {}
-    for d in range(stops[0], -1, -1):
-        lane = d + 1 <= stops[0] and d + 1 not in stops
-        at = ready[d + 1] + LANE if lane else 0.0
-        express = d in stops and d != stops[0]
-        hop = 1
-        if express:
-            last = stops[stops.index(d) - 1]
-            at = max(at, ready[last] + EXPRESS + PER_CHIP * (last - d))
-        if d in stops and d > 0:
-            hop = d - stops[stops.index(d) + 1]
-        ready[d] = at
-        roles[d] = (lane, last if express else None, hop, at)
-    return roles
-
-
-PLANS = tuple(side_plan(g) for g in GAPS)
-ORDER = sorted(((PLANS[s][d][3], -d, s) for s in range(2) for d in PLANS[s] if d > 0))
-OFFSETS = sorted({1} | set(GAPS[0]) | set(GAPS[1]))
-SLOTS = max(sum(g) for g in GAPS) + 1
+GAPS = ((2, 3, 3, 4, 4), (2, 3, 3, 4, 3))
+STOPS = tuple(tuple(sum(g[i:]) for i in range(len(g) + 1)) for g in GAPS)
+BETWEEN = tuple([(i, j) for i in range(1, len(g) + 1) for j in range(1, g[i - 1])] for g in GAPS)
+REACH = max(max(g) for g in GAPS) - 1
+OFFSETS = sorted(set(range(1, REACH + 1)) | set(GAPS[0]) | set(GAPS[1]))
+SLICES = max(len(b) for b in BETWEEN)
+STEPS = max(len(g) for g in GAPS)
 
 
 def dot(a, b, dims=((1,), (0,)), precision=None):
@@ -65,8 +44,8 @@
            lo, tg, gg, gpi_o,
            picked, gate, tok, og, win, wout, gpi,
            rows_s, sc_s, rows_r, sc_r, eo_s, ir_s, eo_r, ir_r, g_v,
-           x_v, xt, hid, bp, perm, perm_t, a_hi, a_lo, a_one, ms, mr,
-           ld_sem, in_ss, in_rs, out_ss, out_rs, sib_ss, sib_rs, m_ss, m_rs):
+           x_v, xt, hid, bp, perm, perm_t, a_hi, a_lo, a_one, xs, bpn, ms, mr,
+           ld_sem, in_ss, in_rs, out_ss, out_rs, sib_ss, sib_rs, m_ss, m_rs, x_ss, x_rs, b_ss, b_rs):
     me = lax.axis_index("expert")
     dp = lax.axis_index("dp")
     z, h = dp // 2, dp % 2
@@ -202,6 +181,13 @@
             xs = dot(perm[...], src[cs * RR:(cs + 1) * RR, :]).astype(BF)
             for q in range(Q):
                 dst[q, cs * R:(cs + 1) * R, :] = xs[q * R:(q + 1) * R, :]
+
+    def along(s, hops):
+        return zdev(hops if s == 0 else -hops)
+
+    def columns(s, d):
+        t = lax.rem(z + (d if s == 0 else -d) + nz, nz)
+        return pl.ds(pl.multiple_of(t * CH, CH), CH)
 
     @pl.when(h == 1)
     def _():
@@ -218,6 +204,11 @@
         slope = cdf + pre * (jnp.exp(-0.5 * pre * pre) * (1.0 / math.sqrt(2.0 * math.pi)))
         for q in range(Q):
             xt[q * W:(q + 1) * W, :] = x_v[q].T
+        for s in range(2):
+            for n, (i, j) in enumerate(BETWEEN[s]):
+                pltpu.make_async_remote_copy(
+                    src_ref=xt.at[columns(s, STOPS[s][i] + j)], dst_ref=xs.at[s, pl.ds(n * CH, CH)],
+                    send_sem=x_ss.at[s], recv_sem=x_rs.at[s], device_id=along(s, j), device_id_type=MESH).start()
         loads[5].wait()
         wait_rows(sc_r, 0, RR, in_rs.at[1, 0])
         wait_rows(sc_r, RR, RR - MR, in_rs.at[1, 1])
@@ -228,50 +219,74 @@
         bp[...] = (back * slope).astype(BF)
         bp_copy.start()
 
-        def own(s, d):
-            t = lax.rem(z + (d if s == 0 else -d) + nz, nz)
-            return dot(xt[pl.ds(pl.multiple_of(t * CH, CH), CH), :], bp[...])
-
-        def message(s, d, u):
-            hop = PLANS[s][d][2]
+        def pass_on(s, j):
+            return pltpu.make_async_remote_copy(
+                src_ref=bpn.at[s, j - 1] if j else bp, dst_ref=bpn.at[s, j],
+                send_sem=b_ss.at[s, j], recv_sem=b_rs.at[s, j], device_id=along(s, 1), device_id_type=MESH)
+
+        def message(s, i, u):
             part = pl.ds(u * SR, SR)
             return pltpu.make_async_remote_copy(
-                src_ref=ms.at[s, d, part], dst_ref=mr.at[s, d, part],
-                send_sem=m_ss.at[s, d, u], recv_sem=m_rs.at[s, d, u],
-                device_id=zdev(hop if s == 0 else -hop), device_id_type=MESH)
-
-        def add(total, s, d, u):
-            message(s, d, u).wait_recv()
-            return total + mr[s, d, u * SR:(u + 1) * SR, :].astype(F32)
-
-        def gathered(total, s, d, u):
-            lane, last, _, _ = PLANS[s][d]
-            if lane:
-                total = add(total, s, d + 1, u)
-            if last is not None:
-                total = add(total, s, last, u)
+                src_ref=ms.at[s, i, part], dst_ref=mr.at[s, i, part],
+                send_sem=m_ss.at[s, i, u], recv_sem=m_rs.at[s, i, u],
+                device_id=along(s, GAPS[s][i]), device_id_type=MESH)
+
+        arrived = [0]
+
+        def need(j):
+            while arrived[0] < j:
+                k = arrived[0]
+                for s in range(2):
+                    pass_on(s, k).wait_recv()
+                    if k + 1 < REACH:
+                        pass_on(s, k + 1).start()
+                arrived[0] += 1
+
+        def others(s, i):
+            total = None
+            for n, (k, j) in enumerate(BETWEEN[s]):
+                if k == i:
+                    need(j)
+                    term = dot(xs[s, n * CH:(n + 1) * CH, :], bpn[s, j - 1])
+                    total = term if total is None else total + term
             return total
 
-        def role(s, d):
-            mine = own(s, d)
+        def add(total, s, i, u):
+            message(s, i - 1, u).wait_recv()
+            return total + mr[s, i - 1, u * SR:(u + 1) * SR, :].astype(F32)
+
+        def stop(s, i):
+            mine = dot(xt[columns(s, STOPS[s][i]), :], bp[...])
+            if i:
+                mine = mine + others(s, i)
             for u in range(NS):
-                total = gathered(mine[u * SR:(u + 1) * SR], s, d, u)
-                ms[s, d, u * SR:(u + 1) * SR, :] = total.astype(BF)
-                message(s, d, u).start()
-
-        for _, nd, s in ORDER:
-            role(s, -nd)
-
-        wait_rows(eo_r, 0, RR, out_rs.at[0])
-        combine_out()
+                total = mine[u * SR:(u + 1) * SR]
+                if i:
+                    total = add(total, s, i, u)
+                ms[s, i, u * SR:(u + 1) * SR, :] = total.astype(BF)
+                message(s, i, u).start()
+
+        for s in range(2):
+            pass_on(s, 0).start()
+        for s in range(2):
+            stop(s, 0)
+        for s in range(2):
+            wait_rows(xs.at[s], 0, len(BETWEEN[s]) * CH, x_rs.at[s])
+        for i in range(1, STEPS):
+            for s in range(2):
+                stop(s, i)
+            if i == STEPS - 2:
+                wait_rows(eo_r, 0, RR, out_rs.at[0])
+                combine_out()
         wait_rows(ir_r, 0, RR, out_rs.at[1])
         combine_grad()
 
-        mine = own(0, 0)
+        mine = dot(xt[columns(0, 0), :], bp[...]) + others(0, STEPS) + others(1, STEPS)
+        need(REACH)
         for u in range(NS):
             total = mine[u * SR:(u + 1) * SR]
             for s in range(2):
-                total = gathered(total, s, 0, u)
+                total = add(total, s, STEPS, u)
             for i in range(u * SR, (u + 1) * SR, min(SR, CH // 2)):
                 part = total[i - u * SR:i - u * SR + min(SR, CH // 2)]
                 if i < CH // 2:
@@ -285,10 +300,12 @@
         hid_copy.wait_send()
         bp_copy.wait_send()
         for s in range(2):
-            for d in PLANS[s]:
-                if d > 0:
-                    for u in range(NS):
-                        message(s, d, u).wait_send()
+            wait_rows(xs.at[s], 0, len(BETWEEN[s]) * CH, x_ss.at[s])
+            for j in range(REACH):
+                pass_on(s, j).wait_send()
+            for i in range(STEPS):
+                for u in range(NS):
+                    message(s, i, u).wait_send()
         gpi_copy.wait_send()
 
     @pl.when(h == 0)
@@ -369,9 +386,9 @@
             buf(RR, W), buf(RR, W), buf(RR, W),
             buf(Q, K, W), buf(D, K), buf(K, F), buf(K, F), buf(RR, RR), buf(RR, RR),
             buf(Q * T, RR), buf(Q * T, RR), buf(Q * T, RR),
-            buf(2, SLOTS, CH, F), buf(2, SLOTS, CH, F),
+            buf(2, SLICES * CH, K), buf(2, REACH, K, F), buf(2, STEPS, CH, F), buf(2, STEPS, CH, F),
             dma((6,)), dma((2,)), dma((2, 2)), dma((2, 2)), dma((2,)), dma((3,)), dma((3,)),
-            dma((2, SLOTS, NS)), dma((2, SLOTS, NS)),
+            dma((2, STEPS, NS)), dma((2, STEPS, NS)), dma((2,)), dma((2,)), dma((2, REACH)), dma((2, REACH)),
         ],
         compiler_params=pltpu.CompilerParams(
             collective_id=0, has_side_effects=True, vmem_limit_bytes=60 * 1024 * 1024),

time: 63.7 us -> 62.2 us (0.976); the launches traced: 62.5 us -> 62 us
  no operation moved by 1% of the time
where the time goes in v3:
time: 62.2 us; the launch traced here: 62 us
  Pallas kernels  61.4 us (99%)
  between operations  0.64 us (1%)
    pallas_call x1, Pallas kernels, body(): pl.pallas_call(functools.partial(kernel, nz), out_shape=shapes, in_specs=...  59.1 us
    pallas_call x1, Pallas kernels, body(): pl.pallas_call(copy_out, out_shape=shapes, in_specs=[vmem] * 4, out_specs...  2.22 us

profile of v3, /device:TPU:1, one launch (start us, length us, event | category | flops | bytes accessed | tf_op | source)
XLA Modules:
  0.0 62.0 jit_solution(8262186160429192367)
XLA Ops:
  0.6 59.1 %moe_layer.1 = (bf16[128,2048]{1,0:T(8,128)(2,1)}, bf16[128,2048]{1,0:T(8,128)(2,1)}, f32[4,16]{1,0:T(4,128)}, f32[32,512]{1,0:T(8,128)}) custom-call(s32[4,16]{1,0:T(4,128)} %bitcast.14, f32[4,16]{1,0:T(4,128)} %bitcast.15, bf16[128,2048]{1,0:T(8,128)(2,1)} %tok_h.1, bf16[128,2048]{1,0:T(8,128)(2,1)} %og_h.1, bf16[2048,512]{1,0:T(8,128)(2,1)} %bitcast.12, ...), custom_call_target="tpu_custom_call" | custom-call | tf_op jit(solution)/shard_map/moe_layer/pallas_call | solution.py:377
  59.8 2.2 %copy_out.1 = (bf16[128,2048]{1,0:T(8,128)(2,1)}, bf16[128,2048]{1,0:T(8,128)(2,1)}, f32[4,16]{1,0:T(4,128)}, f32[32,512]{1,0:T(8,128)}) custom-call(bf16[128,2048]{1,0:T(8,128)(2,1)} %get-tuple-element.12.a, bf16[128,2048]{1,0:T(8,128)(2,1)} %get-tuple-element.13.b, f32[4,16]{1,0:T(4,128)} %get-tuple-element.14.c, f32[32,512]{1,0:T(8,128)} %get-tuple-element.15.d), custom_call_target="tpu_custom_call" | custom-call | tf_op jit(solution)/shard_map/copy_out/pallas_call | solution.py:397

commit v4 on v3

--- a/solution.py
+++ b/solution.py
@@ -41,11 +41,11 @@
 
 
 def kernel(nz, picked_h, gate_h, tok_h, og_h, win_h, wout_h,
-           lo, tg, gg, gpi_o,
-           picked, gate, tok, og, win, wout, gpi,
+           lo_h, tg_h, gg_h, gpi_h,
+           picked, gate, tok, og, win, wout, lo, tg, gg, gpi,
            rows_s, sc_s, rows_r, sc_r, eo_s, ir_s, eo_r, ir_r, g_v,
            x_v, xt, hid, bp, perm, perm_t, a_hi, a_lo, a_one, xs, bpn, ms, mr,
-           ld_sem, in_ss, in_rs, out_ss, out_rs, sib_ss, sib_rs, m_ss, m_rs, x_ss, x_rs, b_ss, b_rs):
+           ld_sem, st_sem, in_ss, in_rs, out_ss, out_rs, sib_ss, sib_rs, m_ss, m_rs, x_ss, x_rs, b_ss, b_rs):
     me = lax.axis_index("expert")
     dp = lax.axis_index("dp")
     z, h = dp // 2, dp % 2
@@ -124,6 +124,10 @@
 
     loads[2].wait()
     rows_s[...] = dot(gather, quarters(tok)).astype(BF)
+    loads[3].wait()
+    grad_rows = dot(gather, quarters(og))
+    sc_s[...] = (w * grad_rows).astype(BF)
+    g_v[...] = grad_rows.astype(BF)
 
     @pl.when(h == 0)
     def _():
@@ -134,11 +138,7 @@
         pl.semaphore_wait(barrier, 2 * E - 1 + 2 * len(OFFSETS))
 
     send_in(0, rows_s, rows_r)
-    loads[3].wait()
-    grad_rows = dot(gather, quarters(og))
-    sc_s[...] = (w * grad_rows).astype(BF)
     send_in(1, sc_s, sc_r)
-    g_v[...] = grad_rows.astype(BF)
 
     i0, i1 = iota((RR, RR), 0), iota((RR, RR), 1)
     to_q = ((i0 >> 2) & 15) * MR + (i0 >> 6) * C + (i0 & 3)
@@ -157,15 +157,21 @@
         for q in range(Q):
             a = slice(q * T, (q + 1) * T)
             lo[:, q * W:(q + 1) * W] = (dot(a_hi[a, :], eo_r[...]) + dot(a_lo[a, :], eo_r[...])).astype(BF)
+        stores[0].start()
         prod = jnp.sum(g_v[...].astype(F32) * eo_r[...].astype(F32), axis=1, keepdims=True)
         sel_t = ((iota((E, RR), 1) >> 4) == iota((E, RR), 0)).astype(F32)
         prod_row = jnp.sum(jnp.where(diag, prod, 0.0), axis=0, keepdims=True)
         by_c = jnp.where((iota((C, RR), 1) & 3) == iota((C, RR), 0), prod_row, 0.0)
         gg[...] = dot(by_c, sel_t, NT, HIGH)
+        stores[2].start()
 
     def combine_grad():
         for q in range(Q):
             tg[:, q * W:(q + 1) * W] = dot(a_one[q * T:(q + 1) * T, :], ir_r[...]).astype(BF)
+        stores[1].start()
+
+    stores = [pltpu.make_async_copy(s, d, st_sem.at[i])
+              for i, (s, d) in enumerate([(lo, lo_h), (tg, tg_h), (gg, gg_h)])]
 
     def to_sib(i, src, dst):
         return pltpu.make_async_remote_copy(
@@ -174,7 +180,8 @@
 
     hid_copy = to_sib(0, hid, hid)
     bp_copy = to_sib(1, bp, bp)
-    gpi_copy = to_sib(2, gpi, gpi_o)
+    gpi_copy = to_sib(2, gpi.at[pl.ds(0, CH // 2)], gpi_h)
+    gpi_own = pltpu.make_async_copy(gpi.at[pl.ds(CH // 2, CH // 2)], gpi_h, st_sem.at[3])
 
     def by_quarter(src, dst):
         for cs in range(2):
@@ -287,14 +294,10 @@
             total = mine[u * SR:(u + 1) * SR]
             for s in range(2):
                 total = add(total, s, STEPS, u)
-            for i in range(u * SR, (u + 1) * SR, min(SR, CH // 2)):
-                part = total[i - u * SR:i - u * SR + min(SR, CH // 2)]
-                if i < CH // 2:
-                    gpi[i:i + part.shape[0], :] = part
-                else:
-                    gpi_o[i - CH // 2:i - CH // 2 + part.shape[0], :] = part
-            if (u + 1) * SR == max(SR, CH // 2):
+            gpi[u * SR:(u + 1) * SR, :] = total
+            if u == max(NS // 2 - 1, 0):
                 gpi_copy.start()
+        gpi_own.start()
         wait_rows(rows_s, 0, RR - MR, in_ss.at[0])
         wait_rows(sc_s, 0, RR - MR, in_ss.at[1])
         hid_copy.wait_send()
@@ -307,6 +310,7 @@
                 for u in range(NS):
                     message(s, i, u).wait_send()
         gpi_copy.wait_send()
+        gpi_own.wait()
 
     @pl.when(h == 0)
     def _():
@@ -351,6 +355,9 @@
             wait_rows(src, 0, RR, out_ss.at[k, 1])
         gpi_copy.wait_recv()
 
+    for c in stores:
+        c.wait()
+
 
 def copy_out(a, b, c, d, oa, ob, oc, od, sem):
     copies = [pltpu.make_async_copy(s, t, sem.at[i]) for i, (s, t) in enumerate(((a, oa), (b, ob), (c, oc), (d, od)))]
@@ -378,16 +385,16 @@
         functools.partial(kernel, nz),
         out_shape=shapes,
         in_specs=[hbm] * 6,
-        out_specs=(vmem,) * 4,
+        out_specs=(hbm,) * 4,
         scratch_shapes=[
             buf(C, E, dtype=jnp.int32), buf(C, E, dtype=F32), buf(T, D), buf(T, D), buf(D, F), buf(F, D),
-            buf(CH // 2, F, dtype=F32),
+            buf(T, D), buf(T, D), buf(C, E, dtype=F32), buf(CH, F, dtype=F32),
             buf(RR, W), buf(RR, W), buf(2 * RR, W), buf(2 * RR, W), buf(2 * RR, W), buf(2 * RR, W),
             buf(RR, W), buf(RR, W), buf(RR, W),
             buf(Q, K, W), buf(D, K), buf(K, F), buf(K, F), buf(RR, RR), buf(RR, RR),
             buf(Q * T, RR), buf(Q * T, RR), buf(Q * T, RR),
             buf(2, SLICES * CH, K), buf(2, REACH, K, F), buf(2, STEPS, CH, F), buf(2, STEPS, CH, F),
-            dma((6,)), dma((2,)), dma((2, 2)), dma((2, 2)), dma((2,)), dma((3,)), dma((3,)),
+            dma((6,)), dma((4,)), dma((2,)), dma((2, 2)), dma((2, 2)), dma((2,)), dma((3,)), dma((3,)),
             dma((2, STEPS, NS)), dma((2, STEPS, NS)), dma((2,)), dma((2,)), dma((2, REACH)), dma((2, REACH)),
         ],
         compiler_params=pltpu.CompilerParams(

time: 62.2 us -> 61.3 us (0.986)
  Pallas kernels: 61.4 us -> 60.5 us
    pallas_call x1, Pallas kernels: 59.1 us -> 58.3 us  [body(): pl.pallas_call(functools.partial(kernel, nz), out_shape=shapes, in_specs=...]
where the time goes in v4:
time: 61.3 us; the launch traced here: 61.2 us
  Pallas kernels  60.5 us (99%)
  between operations  0.64 us (1%)
    pallas_call x1, Pallas kernels, body(): pl.pallas_call(functools.partial(kernel, nz), out_shape=shapes, in_specs=...  58.3 us
    pallas_call x1, Pallas kernels, body(): pl.pallas_call(copy_out, out_shape=shapes, in_specs=[vmem] * 4, out_specs...  2.22 us

profile of v4, /device:TPU:1, one launch (start us, length us, event | category | flops | bytes accessed | tf_op | source)
XLA Modules:
  0.0 61.2 jit_solution(16054536774746697313)
XLA Ops:
  0.6 58.3 %moe_layer.1 = (bf16[128,2048]{1,0:T(8,128)(2,1)}, bf16[128,2048]{1,0:T(8,128)(2,1)}, f32[4,16]{1,0:T(4,128)}, f32[32,512]{1,0:T(8,128)}) custom-call(s32[4,16]{1,0:T(4,128)} %bitcast.14, f32[4,16]{1,0:T(4,128)} %bitcast.15, bf16[128,2048]{1,0:T(8,128)(2,1)} %tok_h.1, bf16[128,2048]{1,0:T(8,128)(2,1)} %og_h.1, bf16[2048,512]{1,0:T(8,128)(2,1)} %bitcast.12, ...), custom_call_target="tpu_custom_call" | custom-call | tf_op jit(solution)/shard_map/moe_layer/pallas_call | solution.py:384
  59.0 2.2 %copy_out.1 = (bf16[128,2048]{1,0:T(8,128)(2,1)}, bf16[128,2048]{1,0:T(8,128)(2,1)}, f32[4,16]{1,0:T(4,128)}, f32[32,512]{1,0:T(8,128)}) custom-call(bf16[128,2048]{1,0:T(8,128)(2,1)} %get-tuple-element.12.a, bf16[128,2048]{1,0:T(8,128)(2,1)} %get-tuple-element.13.b, f32[4,16]{1,0:T(4,128)} %get-tuple-element.14.c, f32[32,512]{1,0:T(8,128)} %get-tuple-element.15.d), custom_call_target="tpu_custom_call" | custom-call | tf_op jit(solution)/shard_map/copy_out/pallas_call | solution.py:404

commit v5 on v4

--- a/solution.py
+++ b/solution.py
@@ -274,9 +274,9 @@
                 message(s, i, u).start()
 
         for s in range(2):
+            stop(s, 0)
+        for s in range(2):
             pass_on(s, 0).start()
-        for s in range(2):
-            stop(s, 0)
         for s in range(2):
             wait_rows(xs.at[s], 0, len(BETWEEN[s]) * CH, x_rs.at[s])
         for i in range(1, STEPS):

time: 61.3 us -> 64.5 us (1.052)
  Pallas kernels: 60.5 us -> 63.7 us
    pallas_call x1, Pallas kernels: 58.3 us -> 61.5 us  [body(): pl.pallas_call(functools.partial(kernel, nz), out_shape=shapes, in_specs=...]
where the time goes in v5:
time: 64.5 us; the launch traced here: 64.4 us
  Pallas kernels  63.7 us (99%)
    pallas_call x1, Pallas kernels, body(): pl.pallas_call(functools.partial(kernel, nz), out_shape=shapes, in_specs=...  61.5 us
    pallas_call x1, Pallas kernels, body(): pl.pallas_call(copy_out, out_shape=shapes, in_specs=[vmem] * 4, out_specs...  2.22 us

profile of v5, /device:TPU:1, one launch (start us, length us, event | category | flops | bytes accessed | tf_op | source)
XLA Modules:
  0.0 64.4 jit_solution(4741676726132270771)
XLA Ops:
  0.6 61.5 %moe_layer.1 = (bf16[128,2048]{1,0:T(8,128)(2,1)}, bf16[128,2048]{1,0:T(8,128)(2,1)}, f32[4,16]{1,0:T(4,128)}, f32[32,512]{1,0:T(8,128)}) custom-call(s32[4,16]{1,0:T(4,128)} %bitcast.14, f32[4,16]{1,0:T(4,128)} %bitcast.15, bf16[128,2048]{1,0:T(8,128)(2,1)} %tok_h.1, bf16[128,2048]{1,0:T(8,128)(2,1)} %og_h.1, bf16[2048,512]{1,0:T(8,128)(2,1)} %bitcast.12, ...), custom_call_target="tpu_custom_call" | custom-call | tf_op jit(solution)/shard_map/moe_layer/pallas_call | solution.py:384
  62.1 2.2 %copy_out.1 = (bf16[128,2048]{1,0:T(8,128)(2,1)}, bf16[128,2048]{1,0:T(8,128)(2,1)}, f32[4,16]{1,0:T(4,128)}, f32[32,512]{1,0:T(8,128)}) custom-call(bf16[128,2048]{1,0:T(8,128)(2,1)} %get-tuple-element.12.a, bf16[128,2048]{1,0:T(8,128)(2,1)} %get-tuple-element.13.b, f32[4,16]{1,0:T(4,128)} %get-tuple-element.14.c, f32[32,512]{1,0:T(8,128)} %get-tuple-element.15.d), custom_call_target="tpu_custom_call" | custom-call | tf_op jit(solution)/shard_map/copy_out/pallas_call | solution.py:404
